TPU v7x, 256 devices: a whole 4x4x8 slice. The times are simulated.
256 devices in a mesh: dom: 64 (over x, z, core), line: 4 (over y).
Axes of the slice: x: 4, y: 4, z: 8, core: 2. Of those that a mesh axis runs over, the one named last changes fastest.
Arguments:
- right_side: float32 [64, 32768], P(None, ('dom', 'line')), may hold values from -18 to 18
- diag_blocks: bfloat16 [64, 64, 32768], P(None, None, ('dom', 'line')), may hold values from -0.5 to 3.5
- lower_blocks: bfloat16 [64, 64, 32768], P(None, None, ('dom', 'line')), may hold values from -0.375 to 0.375
- upper_blocks: bfloat16 [64, 64, 32768], P(None, None, ('dom', 'line')), may hold values from -0.375 to 0.375
- face_blocks: bfloat16 [4, 64, 64, 32768], P(None, None, None, ('dom', 'line')), may hold values from -0.75 to 0.75
- face_nbr: int32 [4, 32768], P(None, ('dom', 'line')), may hold values from 0 to 160, as said below
- send_list: int32 [2, 4096], P(None, ('dom', 'line')), may hold values from 0 to 127
- inv_blocks: bfloat16 [64, 64, 32768], P(None, None, ('dom', 'line')), may hold values from -0.75 to 0.75
- fwd_blocks: bfloat16 [64, 64, 32768], P(None, None, ('dom', 'line')), may hold values from -0.625 to 0.625
- bwd_blocks: bfloat16 [64, 64, 32768], P(None, None, ('dom', 'line')), may hold values from -0.625 to 0.625
Outputs:
- update: float32 [64, 32768], P(None, ('dom', 'line'))
- hessenberg: float32 [4, 3], replicated
Inputs may be any that keep to these rules, and one draw needn't show every extreme that they name: `face_nbr`: slots 128 to 159 name values received from the neighbouring partitions and slot 160 is the zero slot.
All inputs are finite; a program needn't handle non-finite values.
Results may differ from a plain program's by a relative error of at most 0.015.
Values may be sent and summed in bfloat16 or wider, within the bound.
A program may use at most 64 MiB of HBM per device.

v0:
```python
import jax
import jax.numpy as jnp
from jax import lax
from jax.sharding import PartitionSpec as P

ITERS = 3
LINES_DEV = 16


HIGHEST = lax.Precision.HIGHEST


def with_halo(cells, sides, width):
    for axis, dim in sides:
        count = lax.axis_size(axis)
        ends = count - 1
        head = lax.slice_in_dim(cells, 0, width, axis=dim)
        tail = lax.slice_in_dim(cells, cells.shape[dim] - width, cells.shape[dim], axis=dim)
        cells = jnp.concatenate(
            [
                lax.ppermute(tail, axis, [(i, (i + 1) % count) for i in range(ends)]),
                cells,
                lax.ppermute(head, axis, [((i + 1) % count, i) for i in range(ends)]),
            ],
            axis=dim,
        )
    return cells


def from_behind(block, axis, distance):
    devices = range(lax.axis_size(axis))
    route = [(i - distance, i) for i in devices if i - distance in devices]
    return lax.ppermute(block, axis, route)


def prefix(array, axis, combine, identity):
    size, place = (lax.axis_size(axis), lax.axis_index(axis))
    everything = jax.tree.map(
        lambda part, kind: lax.all_gather(part.astype(kind), axis),
        array,
        (jnp.bfloat16, jnp.bfloat16),
    )
    start = jax.tree.map(
        lambda part, zero: jnp.broadcast_to(jnp.asarray(zero, part.dtype), part.shape),
        array,
        identity,
    )

    def lap(k, before):
        reached = k < place
        new = combine(
            before, jax.tree.map(lambda part, own: part[k].astype(own.dtype), everything, array)
        )
        return jax.tree.map(lambda a, b: jnp.where(reached, a, b), new, before)

    return lax.fori_loop(0, size, lap, start)


def entering_2(array, axis, join, neutral):
    count = lax.axis_size(axis)
    place = lax.axis_index(axis)
    ahead = count - 1 - place
    gathered = jax.tree.map(
        lambda a, kind: lax.all_gather(a.astype(kind), axis),
        array,
        jax.tree.map(lambda a: jnp.bfloat16 if a.dtype == jnp.float32 else a.dtype, array),
    )
    state = jax.tree.map(lambda a, e: jnp.zeros_like(a) + jnp.asarray(e, a.dtype), array, neutral)

    def one(lap, state):
        source = count - 1 - lap
        return join(
            state,
            jax.tree.map(
                lambda a, own: lax.dynamic_index_in_dim(a, source, 0, False).astype(own.dtype),
                gathered,
                array,
            ),
        )

    return lax.fori_loop(0, ahead, one, state)


def apply_blocks(blocks, rounded):
    return jnp.einsum("ije,je->ie", blocks, rounded, preferred_element_type=jnp.float32)


def couple(blocks, carried):
    return jnp.einsum("ijl,jl->il", blocks.astype(jnp.float32), carried, precision=HIGHEST)


def compose(earlier, latter):
    matrix_early, vector_early = earlier
    matrix_late, vector_late = latter
    joined = jnp.einsum("ijl,jkl->ikl", matrix_late, matrix_early, precision=HIGHEST)
    return (joined, couple(matrix_late, vector_early) + vector_late)


def sweep_down(source, blocks, inflow):
    carried = inflow
    values = []
    for position in range(source.shape[1]):
        carried = source[:, position] - couple(blocks[:, :, position], carried)
        values.append(carried)
    return jnp.stack(values, axis=1)


def sweep_up(source, blocks, inflow):
    carried = inflow
    values = []
    for position in reversed(range(source.shape[1])):
        carried = source[:, position] - couple(blocks[:, :, position], carried)
        values.append(carried)
    return jnp.stack(values[::-1], axis=1)


def transfer(blocks, order):
    block_size, line_count = (blocks.shape[0], blocks.shape[3])
    matrix = jnp.broadcast_to(
        jnp.eye(block_size, dtype=jnp.float32)[:, :, None], (block_size, block_size, line_count)
    )
    for position in order:
        matrix = -jnp.einsum(
            "ijl,jkl->ikl", blocks[:, :, position].astype(jnp.float32), matrix, precision=HIGHEST
        )
    return matrix


def squared(vector):
    return lax.psum(jnp.sum(vector * vector), ("dom", "line"))


def shards(
    right_side,
    diag_blocks,
    lower_blocks,
    upper_blocks,
    face_blocks,
    face_nbr,
    send_list,
    inv_blocks,
    fwd_blocks,
    bwd_blocks,
):
    block_size, elements = right_side.shape
    line_count = LINES_DEV
    positions = elements // line_count
    grid_shape = (block_size, positions, line_count)
    forward_couple = fwd_blocks.reshape(block_size, block_size, positions, line_count)
    backward_couple = bwd_blocks.reshape(block_size, block_size, positions, line_count)
    zero_state = jnp.zeros((block_size, line_count), jnp.float32)
    forward_map = transfer(forward_couple, range(positions))
    backward_map = transfer(backward_couple, reversed(range(positions)))
    eye_stack = jnp.broadcast_to(
        jnp.eye(block_size, dtype=jnp.float32)[:, :, None], (block_size, block_size, line_count)
    )
    start_norm = jnp.sqrt(squared(right_side))
    krylov = [right_side / start_norm]
    search = []
    hessenberg = jnp.zeros((ITERS + 1, ITERS), jnp.float32)
    for iteration in range(ITERS):
        source = apply_blocks(inv_blocks, krylov[iteration].astype(jnp.bfloat16)).reshape(
            grid_shape
        )
        provisional = sweep_down(source, forward_couple, zero_state)
        entering = prefix(
            (forward_map, provisional[:, -1]), "line", compose, (eye_stack, zero_state)
        )
        forward = sweep_down(source, forward_couple, entering[1])
        second = sweep_up(forward, backward_couple, zero_state)
        entering = entering_2(
            (backward_map, second[:, 0]), "line", compose, (eye_stack, zero_state)
        )
        result = sweep_up(forward, backward_couple, entering[1])
        direction = result.reshape(block_size, elements)
        search.append(direction)
        rounded = direction.astype(jnp.bfloat16)
        padded = with_halo(rounded.reshape(grid_shape), (("line", 1),), 1)
        to_right = rounded[:, send_list[0]]
        to_left = rounded[:, send_list[1]]
        from_left = from_behind(to_right, "dom", 1)
        from_right = from_behind(to_left, "dom", -1)
        summed = apply_blocks(diag_blocks, rounded)
        summed = summed + apply_blocks(lower_blocks, padded[:, :-2].reshape(block_size, elements))
        summed = summed + apply_blocks(upper_blocks, padded[:, 2:].reshape(block_size, elements))
        empty_slot = jnp.zeros((block_size, 1), jnp.bfloat16)
        extended = jnp.concatenate([rounded, from_left, from_right, empty_slot], axis=1)
        neighbours = extended[:, face_nbr]
        summed = summed + jnp.einsum(
            "fije,jfe->ie", face_blocks, neighbours, preferred_element_type=jnp.float32
        )
        product_vec = summed
        for column in range(iteration + 1):
            weight_ij = lax.psum(jnp.sum(product_vec * krylov[column]), ("dom", "line"))
            product_vec = product_vec - weight_ij * krylov[column]
            hessenberg = hessenberg.at[column, iteration].set(weight_ij)
        height = jnp.sqrt(squared(product_vec))
        hessenberg = hessenberg.at[iteration + 1, iteration].set(height)
        if iteration + 1 < ITERS:
            krylov.append(product_vec / height)
    normal = jnp.dot(hessenberg.T, hessenberg, precision=HIGHEST)
    target = start_norm * hessenberg[0]
    factor = jnp.linalg.cholesky(normal)
    coeffs = jax.scipy.linalg.cho_solve((factor, True), target)
    update = coeffs[0] * search[0]
    for iteration in range(1, ITERS):
        update = update + coeffs[iteration] * search[iteration]
    return (update, hessenberg)


def solution(mesh):
    in_specs = (
        P(None, ("dom", "line")),
        P(None, None, ("dom", "line")),
        P(None, None, ("dom", "line")),
        P(None, None, ("dom", "line")),
        P(None, None, None, ("dom", "line")),
        P(None, ("dom", "line")),
        P(None, ("dom", "line")),
        P(None, None, ("dom", "line")),
        P(None, None, ("dom", "line")),
        P(None, None, ("dom", "line")),
    )
    out_specs = (P(None, ("dom", "line")), P())
    return jax.shard_map(shards, mesh=mesh, in_specs=in_specs, out_specs=out_specs, check_vma=False)
```

profile of v0, /device:TPU:1, one launch (start us, length us, event | category | flops | bytes accessed | tf_op | source)
XLA Modules:
  0.0 1134.6 jit_solution(403124529077822233)
XLA Ops:
  0.7 4.0 copy.34
  7.3 3.8 copy.36
  14.8 81.4 %psum.70 = f32[]{:T(128)} all-reduce(f32[]{:T(128)} %multiply_reduce_fusion.6), channel_id=1, replica_groups=mesh['dom'=64,'line'=4] {'dom','line'}, use_global_device_ids=true, to_apply=%region_1.0 | all-reduce | flops 1 | bytes 8 | tf_op jit(solution)/shard_map/psum | solution.py:130
  112.7 9.0 all-gather.8
  127.8 12.8 %all-gather = bf16[256,64,16]{1,2,0:T(8,128)(2,1)S(1)} all-gather(bf16[64,64,16]{1,2,0:T(8,128)(2,1)S(1)} %copy.35), channel_id=2, replica_groups=mesh['dom'=64,'line'=4] {'line'}, dimensions={0}, use_global_device_ids=true | all-gather | bytes 655360 | tf_op jit(solution)/shard_map/all_gather | solution.py:39
  164.1 9.1 all-gather.9
  177.3 11.0 all-gather.2
  205.8 14.1 %collective-permute-start.2 = (bf16[64,16]{0,1:T(8,128)(2,1)S(1)}, bf16[64,16]{0,1:T(8,128)(2,1)}, u32[]{:S(2)}, u32[]{:S(2)}) collective-permute-start(bf16[64,16]{0,1:T(8,128)(2,1)S(1)} %bitcast.1672), channel_id=1, source_target_pairs={{0,4},{4,8},{8,12},{12,16},{16,20},{20,24},{24,28},{28,32},{32,36}... | collective-permute-start | bytes 6152 | tf_op jit(solution)/shard_map/ppermute | solution.py:33
  238.4 75.1 %psum.71 = f32[]{:T(128)} all-reduce(f32[]{:T(128)} %get-tuple-element.840), channel_id=1, replica_groups=mesh['dom'=64,'line'=4] {'dom','line'}, use_global_device_ids=true, to_apply=%region_7.8 | all-reduce | flops 1 | bytes 8 | tf_op jit(solution)/shard_map/psum | solution.py:194
  314.8 73.5 %psum.72 = f32[]{:T(128)} all-reduce(f32[]{:T(128)} %multiply_reduce_fusion.5), channel_id=1, replica_groups=mesh['dom'=64,'line'=4] {'dom','line'}, use_global_device_ids=true, to_apply=%region_9.10 | all-reduce | flops 1 | bytes 8 | tf_op jit(solution)/shard_map/psum | solution.py:130
  405.4 9.0 all-gather.10
  437.9 9.1 all-gather.11
  466.6 9.7 collective-permute-start.6
  494.8 75.0 %psum.73 = f32[]{:T(128)} all-reduce(f32[]{:T(128)} %get-tuple-element.836), channel_id=1, replica_groups=mesh['dom'=64,'line'=4] {'dom','line'}, use_global_device_ids=true, to_apply=%region_15.16 | all-reduce | flops 1 | bytes 8 | tf_op jit(solution)/shard_map/psum | solution.py:194
  571.2 73.5 %psum.74 = f32[]{:T(128)} all-reduce(f32[]{:T(128)} %get-tuple-element.834), channel_id=1, replica_groups=mesh['dom'=64,'line'=4] {'dom','line'}, use_global_device_ids=true, to_apply=%region_17.18 | all-reduce | flops 1 | bytes 8 | tf_op jit(solution)/shard_map/psum | solution.py:194
  645.9 73.6 %psum.75 = f32[]{:T(128)} all-reduce(f32[]{:T(128)} %multiply_reduce_fusion.3), channel_id=1, replica_groups=mesh['dom'=64,'line'=4] {'dom','line'}, use_global_device_ids=true, to_apply=%region_19.20 | all-reduce | flops 1 | bytes 8 | tf_op jit(solution)/shard_map/psum | solution.py:130
  736.5 9.0 all-gather.12
  769.1 9.1 all-gather.13
  798.3 10.3 collective-permute-start.10
  817.1 3.3 fusion.17
  821.0 74.4 %psum.76 = f32[]{:T(128)} all-reduce(f32[]{:T(128)} %get-tuple-element.830), channel_id=1, replica_groups=mesh['dom'=64,'line'=4] {'dom','line'}, use_global_device_ids=true, to_apply=%region_26.27 | all-reduce | flops 1 | bytes 8 | tf_op jit(solution)/shard_map/psum | solution.py:194
  896.7 73.5 %psum.77 = f32[]{:T(128)} all-reduce(f32[]{:T(128)} %get-tuple-element.828), channel_id=1, replica_groups=mesh['dom'=64,'line'=4] {'dom','line'}, use_global_device_ids=true, to_apply=%region_28.29 | all-reduce | flops 1 | bytes 8 | tf_op jit(solution)/shard_map/psum | solution.py:194
  971.5 73.4 %psum.78 = f32[]{:T(128)} all-reduce(f32[]{:T(128)} %multiply_reduce_fusion.1), channel_id=1, replica_groups=mesh['dom'=64,'line'=4] {'dom','line'}, use_global_device_ids=true, to_apply=%region_30.31 | all-reduce | flops 1 | bytes 8 | tf_op jit(solution)/shard_map/psum | solution.py:194
  1048.8 74.1 %psum.79 = f32[]{:T(128)} all-reduce(f32[]{:T(128)} %multiply_reduce_fusion), channel_id=1, replica_groups=mesh['dom'=64,'line'=4] {'dom','line'}, use_global_device_ids=true, to_apply=%region_32.33 | all-reduce | flops 1 | bytes 8 | tf_op jit(solution)/shard_map/psum | solution.py:130
  (497 shorter events, 268.5 us)
Async XLA Ops:
  7.3 89.5 %copy-start = (bf16[64,64,128]{2,1,0:T(8,128)(2,1)S(1)}, bf16[64,64,128]{2,1,0:T(8,128)(2,1)}, u32[]{:S(2)}) copy-start(bf16[64,64,128]{2,1,0:T(8,128)(2,1)} %param.47) | copy-start | bytes 3145732
  12.6 109.2 %copy-start.10 = (f32[64,64,16]{0,1,2:T(8,128)S(1)}, f32[64,64,16]{0,1,2:T(8,128)}, u32[]{:S(2)}) copy-start(f32[64,64,16]{0,1,2:T(8,128)} %fusion.43) | copy-start | bytes 786436
  101.0 23.8 %copy-start.8 = (bf16[64,64,128]{1,0,2:T(8,128)(2,1)S(1)}, bf16[64,64,128]{1,0,2:T(8,128)(2,1)}, u32[]{:S(2)}) copy-start(bf16[64,64,128]{1,0,2:T(8,128)(2,1)} %copy-done.7) | copy-start | bytes 3145732
  189.9 32.7 %copy-start.28 = (s32[4,128]{1,0:T(4,128)S(1)}, s32[4,128]{1,0:T(4,128)}, u32[]{:S(2)}) copy-start(s32[4,128]{1,0:T(4,128)} %param.45) | copy-start | bytes 6148
  189.9 34.1 %copy-start.30 = (s32[2]{0:T(128)S(1)}, s32[2]{0:T(128)}, u32[]{:S(2)}) copy-start(s32[2]{0:T(128)} %constant.454.clone.1) | copy-start | bytes 28
  202.6 24.9 %collective-permute-start = (bf16[64,1,16]{0,2,1:T(8,128)(2,1)S(1)}, bf16[64,1,16]{0,2,1:T(8,128)(2,1)S(1)}, u32[]{:S(2)}, u32[]{:S(2)}) collective-permute-start(bf16[64,1,16]{0,2,1:T(8,128)(2,1)S(1)} %get-tuple-element.858), channel_id=1, source_target_pairs={{0,1},{1,2},{2,3},{4,5},{5,6},{6,7},{8,9},{9,10},{10,11},{12,13},{... | collective-permute-start | bytes 6152 | tf_op jit(solution)/shard_map/ppermute | solution.py:21
  203.9 23.6 %collective-permute-start.1 = (bf16[64,1,16]{0,2,1:T(8,128)(2,1)S(1)}, bf16[64,1,16]{0,2,1:T(8,128)(2,1)S(1)}, u32[]{:S(2)}, u32[]{:S(2)}) collective-permute-start(bf16[64,1,16]{0,2,1:T(8,128)(2,1)S(1)} %get-tuple-element.859), channel_id=1, source_target_pairs={{1,0},{2,1},{3,2},{5,4},{6,5},{7,6},{9,8},{10,9},{11,10},{13,12},{... | collective-permute-start | bytes 6152 | tf_op jit(solution)/shard_map/ppermute | solution.py:23
  205.8 21.9 %collective-permute-start.2 = (bf16[64,16]{0,1:T(8,128)(2,1)S(1)}, bf16[64,16]{0,1:T(8,128)(2,1)}, u32[]{:S(2)}, u32[]{:S(2)}) collective-permute-start(bf16[64,16]{0,1:T(8,128)(2,1)S(1)} %bitcast.1672), channel_id=1, source_target_pairs={{0,4},{4,8},{8,12},{12,16},{16,20},{20,24},{24,28},{28,32},{32,36}... | collective-permute-start | bytes 6152 | tf_op jit(solution)/shard_map/ppermute | solution.py:33
  220.5 7.2 collective-permute-start.3
  461.2 25.2 %copy-start.15 = (f32[64,8,16]{0,2,1:T(8,128)}, f32[64,8,16]{0,2,1:T(8,128)S(1)}, u32[]{:S(2)}) copy-start(f32[64,8,16]{0,2,1:T(8,128)S(1)} %constant_dynamic-update-slice_fusion.8) | copy-start | bytes 98308
  462.7 18.5 %collective-permute-start.4 = (bf16[64,1,16]{0,2,1:T(8,128)(2,1)S(1)}, bf16[64,1,16]{0,2,1:T(8,128)(2,1)S(1)}, u32[]{:S(2)}, u32[]{:S(2)}) collective-permute-start(bf16[64,1,16]{0,2,1:T(8,128)(2,1)S(1)} %get-tuple-element.854), channel_id=1, source_target_pairs={{0,1},{1,2},{2,3},{4,5},{5,6},{6,7},{8,9},{9,10},{10,11},{12,13},{... | collective-permute-start | bytes 6152 | tf_op jit(solution)/shard_map/ppermute | solution.py:21
  465.3 16.5 %collective-permute-start.5 = (bf16[64,1,16]{0,2,1:T(8,128)(2,1)S(1)}, bf16[64,1,16]{0,2,1:T(8,128)(2,1)}, u32[]{:S(2)}, u32[]{:S(2)}) collective-permute-start(bf16[64,1,16]{0,2,1:T(8,128)(2,1)S(1)} %get-tuple-element.855), channel_id=1, source_target_pairs={{1,0},{2,1},{3,2},{5,4},{6,5},{7,6},{9,8},{10,9},{11,10},{13,12},{... | collective-permute-start | bytes 6152 | tf_op jit(solution)/shard_map/ppermute | solution.py:23
  466.6 19.8 %collective-permute-start.6 = (bf16[64,16]{0,1:T(8,128)(2,1)S(1)}, bf16[64,16]{0,1:T(8,128)(2,1)S(1)}, u32[]{:S(2)}, u32[]{:S(2)}) collective-permute-start(bf16[64,16]{0,1:T(8,128)(2,1)S(1)} %bitcast.1677), channel_id=1, source_target_pairs={{0,4},{4,8},{8,12},{12,16},{16,20},{20,24},{24,28},{28,32},{32,36}... | collective-permute-start | bytes 6152 | tf_op jit(solution)/shard_map/ppermute | solution.py:33
  476.3 10.7 collective-permute-start.7
  780.0 31.5 %copy-start.1 = (bf16[64,64,128]{2,1,0:T(8,128)(2,1)S(1)}, bf16[64,64,128]{2,1,0:T(8,128)(2,1)}, u32[]{:S(2)}) copy-start(bf16[64,64,128]{2,1,0:T(8,128)(2,1)} %param.41) | copy-start | bytes 3145732
  782.2 32.5 %copy-start.2 = (bf16[64,64,128]{2,1,0:T(8,128)(2,1)S(1)}, bf16[64,64,128]{2,1,0:T(8,128)(2,1)}, u32[]{:S(2)}) copy-start(bf16[64,64,128]{2,1,0:T(8,128)(2,1)} %param.42) | copy-start | bytes 3145732
  789.7 25.5 %copy-start.3 = (bf16[64,64,128]{2,1,0:T(8,128)(2,1)S(1)}, bf16[64,64,128]{2,1,0:T(8,128)(2,1)}, u32[]{:S(2)}) copy-start(bf16[64,64,128]{2,1,0:T(8,128)(2,1)} %param.43) | copy-start | bytes 3145732
  793.4 22.1 %copy-start.25 = (bf16[161]{0:T(256)(128)(2,1)S(1)}, bf16[161]{0:T(256)(128)(2,1)}, u32[]{:S(2)}) copy-start(bf16[161]{0:T(256)(128)(2,1)} %pad.59.clone) | copy-start | bytes 970
  794.3 21.4 %copy-start.22 = (s32[1024]{0:T(1024)S(1)}, s32[1024]{0:T(1024)}, u32[]{:S(2)}) copy-start(s32[1024]{0:T(1024)} %copy-done.21) | copy-start | bytes 12292
  795.0 19.6 %collective-permute-start.8 = (bf16[64,1,16]{0,2,1:T(8,128)(2,1)S(1)}, bf16[64,1,16]{0,2,1:T(8,128)(2,1)S(1)}, u32[]{:S(2)}, u32[]{:S(2)}) collective-permute-start(bf16[64,1,16]{0,2,1:T(8,128)(2,1)S(1)} %get-tuple-element.850), channel_id=1, source_target_pairs={{0,1},{1,2},{2,3},{4,5},{5,6},{6,7},{8,9},{9,10},{10,11},{12,13},{... | collective-permute-start | bytes 6152 | tf_op jit(solution)/shard_map/ppermute | solution.py:21
  797.0 17.6 %collective-permute-start.9 = (bf16[64,1,16]{0,2,1:T(8,128)(2,1)S(1)}, bf16[64,1,16]{0,2,1:T(8,128)(2,1)S(1)}, u32[]{:S(2)}, u32[]{:S(2)}) collective-permute-start(bf16[64,1,16]{0,2,1:T(8,128)(2,1)S(1)} %get-tuple-element.851), channel_id=1, source_target_pairs={{1,0},{2,1},{3,2},{5,4},{6,5},{7,6},{9,8},{10,9},{11,10},{13,12},{... | collective-permute-start | bytes 6152 | tf_op jit(solution)/shard_map/ppermute | solution.py:23
  798.3 17.2 %collective-permute-start.10 = (bf16[64,16]{0,1:T(8,128)(2,1)S(1)}, bf16[64,16]{0,1:T(8,128)(2,1)S(1)}, u32[]{:S(2)}, u32[]{:S(2)}) collective-permute-start(bf16[64,16]{0,1:T(8,128)(2,1)S(1)} %bitcast.1675), channel_id=1, source_target_pairs={{0,4},{4,8},{8,12},{12,16},{16,20},{20,24},{24,28},{28,32},{32,36}... | collective-permute-start | bytes 6152 | tf_op jit(solution)/shard_map/ppermute | solution.py:33
  808.6 6.9 collective-permute-start.11
  817.1 314.6 %copy-start.16 = (f32[64,8,16]{0,2,1:T(8,128)S(1)}, f32[64,8,16]{0,2,1:T(8,128)}, u32[]{:S(2)}) copy-start(f32[64,8,16]{0,2,1:T(8,128)} %copy-done.15) | copy-start | bytes 98308
  (19 other events, 147.0 us)
where the time goes:
time: 1150 us; the launch traced here: 1130 us
  blocking collectives  825 us (72%)
  matrix products  138 us (12%)
  other arithmetic  77.9 us (7%)
  starting transfers between devices  49.9 us (4%)
  local copies, waits for them, and re-layouts  36.1 us (3%)
    psum x6, blocking collectives, shards(): weight_ij = lax.psum(jnp.sum(product_vec * krylov[column]), ('dom', 'line'))  445 us
    psum x4, blocking collectives, squared(): return lax.psum(jnp.sum(vector * vector), ('dom', 'line'))  303 us
    dot_general x113, matrix products, couple(): jnp.einsum('ijl,jl->il', blocks.astype(jnp.float32), carried, precision=H...  125 us
    ppermute x6, starting transfers between devices, from_behind(): return lax.ppermute(block, axis, route)  40 us
    all_gather x4, blocking collectives, prefix(): lax.all_gather(part.astype(kind), axis)  39.9 us
    all_gather x4, blocking collectives, entering_2(): lax.all_gather(a.astype(kind), axis)  38.1 us
    sub x42, other arithmetic, sweep_down(): carried = source[:, position] - couple(blocks[:, :, position], carried)  28.2 us
  transfers between devices with their start and end apart: 12, of which 0 were waited for; matrix products, arithmetic and copies ran while one was open for 2% of the time, Pallas kernels for 0%

commit v1 on v0

v1 whole, which is shorter than its diff:
```python
import functools

import jax
import jax.numpy as jnp
from jax import lax
from jax.experimental import pallas as pl
from jax.experimental.pallas import tpu as pltpu
from jax.sharding import PartitionSpec as P

MESH = pl.DeviceIdType.MESH
F32 = jnp.float32
BF16 = jnp.bfloat16
ITERS = 3
B = 64
E = 128
LINES = 16
Q = 8
HALF = Q // 2
HALO = 16
FACES = 4
START_SCALE = 2.0**-15
W_SCALE = 2.0**-24


def iota(shape, dim):
    return lax.broadcasted_iota(jnp.int32, shape, dim)


def merge_rows(parts):
    sub = iota((8, E), 0)

    def keeps(shift, bases):
        mask = sub == bases[0]
        for base in bases[1:]:
            mask = mask | (sub == base)
        return mask

    def join(a, b, roll, mask_a):
        sel_here = jnp.where(mask_a, a, b)
        shifted = keepers[id(mask_a)]
        sel_there = jnp.where(shifted, a, b)
        return sel_here + pltpu.roll(sel_there, roll, 0)

    keepers = {}

    def level(mask_rows, roll):
        mask = keeps(roll, mask_rows)
        moved = keeps(roll, [(row - roll) % 8 for row in mask_rows])
        keepers[id(mask)] = moved
        return mask

    out = {}

    def quad(lo, hi, first):
        rows = [(first + r) % 8 for r in range(4)]
        return join(parts[lo], parts[hi], 4, masks4[first % 8])

    masks4 = {f: level([(f + r) % 8 for r in range(4)], 4) for f in (0, 6, 7, 5)}
    mask_23 = level([2, 3, 6, 7], 2)
    d_odd = join(quad(3, 7, 0), quad(1, 5, 6), 2, mask_23)
    mask_12 = level([1, 2, 5, 6], 2)
    d_even = join(quad(2, 6, 7), quad(0, 4, 5), 2, mask_12)
    mask_odd = level([1, 3, 5, 7], 1)
    return join(d_odd, d_even, 1, mask_odd)


def fold(array):
    groups = [array[8 * r : 8 * r + 8] for r in range(8)]
    while len(groups) > 1:
        groups = [a + b for a, b in zip(groups[::2], groups[1::2])]
    return groups[0]


def kernel(
    sizes,
    right_hbm,
    nbr_hbm,
    send_hbm,
    diag_hbm,
    lower_hbm,
    upper_hbm,
    face_hbm,
    inv_hbm,
    fwd_hbm,
    bwd_hbm,
    update_ref,
    hess_ref,
    right_ref,
    nbr_ref,
    send_ref,
    diag,
    lower,
    upper,
    face,
    inv,
    fwd,
    bwd,
    turned,
    prefix_map,
    chunk_map,
    both_map,
    got_map,
    inflow_map,
    pick,
    send_pick,
    lists,
    vecs,
    source,
    state,
    keep,
    ends,
    got_ends,
    halo_out,
    got_halo,
    part,
    got_a,
    got_b,
    load_sem,
    map_send,
    map_recv,
    end_send,
    end_recv,
    halo_send,
    halo_recv,
    sum_send,
    sum_recv,
):
    n_dom, n_line, high, low = sizes
    n_a, n_b = n_line * high, low
    dom = lax.axis_index("dom")
    line = lax.axis_index("line")
    dom_high = dom // low
    dom_low = dom % low
    place_a = line * high + dom_high

    loads = []
    for slot, (src, dst) in enumerate(
        (
            (fwd_hbm, fwd),
            (bwd_hbm, bwd),
            (right_hbm, right_ref),
            (nbr_hbm, nbr_ref),
            (send_hbm, send_ref),
            (inv_hbm, inv),
            (diag_hbm, diag),
            (upper_hbm, upper),
            (lower_hbm, lower),
            (face_hbm, face),
        )
    ):
        copy = pltpu.make_async_copy(src, dst, load_sem.at[slot])
        copy.start()
        loads.append(copy)

    def around(count, off):
        return min(off, count - off)

    def offsets(first, second):
        pairs = [(a, b) for a in range(first) for b in range(second) if a or b]
        return sorted(pairs, key=lambda p: -around(first, p[0]) - around(second, p[1]))

    peers_a = [
        {"dom": (dom_high + b) % high * low + dom_low, "line": (line + a) % n_line} for a, b in offsets(n_line, high)
    ]
    pairs = low // 2
    peers_b = [
        {"dom": dom_high * low + (dom_low // 2 + a) % pairs * 2 + (dom_low % 2 + b) % 2, "line": line}
        for a, b in offsets(pairs, 2)
    ]

    def peer_line(off):
        return {"dom": dom, "line": (line + off + n_line) % n_line}

    def peer_dom(off):
        return {"dom": (dom + off + n_dom) % n_dom, "line": line}

    inflow_map[...] = jnp.zeros_like(inflow_map)

    barrier = pltpu.get_barrier_semaphore()
    partners = peers_a + peers_b + [peer_dom(1), peer_dom(-1)]
    for partner in partners:
        pl.semaphore_signal(barrier, inc=1, device_id=partner, device_id_type=MESH)

    lane = iota((B, E), 1)
    lane8 = iota((8, E), 1)
    position = lane // LINES

    pending = []

    def sum_start(which, rows):
        rows = list(rows) + [jnp.zeros((8, E), F32)] * (8 - len(rows))
        part[which] = merge_rows(rows)
        got_a[which, place_a] = part[which]
        for peer in peers_a:
            pltpu.make_async_remote_copy(
                src_ref=part.at[which],
                dst_ref=got_a.at[which, place_a],
                send_sem=sum_send.at[which],
                recv_sem=sum_recv.at[which],
                device_id=peer,
                device_id_type=MESH,
            ).start()

    def whole_wait(ref, sem):
        pltpu.make_async_copy(ref, ref, sem).wait()

    def sum_middle(which):
        whole_wait(got_a.at[which, pl.ds(0, n_a - 1)], sum_recv.at[which])
        total = got_a[which, 0]
        for slot in range(1, n_a):
            total = total + got_a[which, slot]
        part[4 + which] = total
        got_b[which, dom_low] = total
        for peer in peers_b:
            pltpu.make_async_remote_copy(
                src_ref=part.at[4 + which],
                dst_ref=got_b.at[which, dom_low],
                send_sem=sum_send.at[4 + which],
                recv_sem=sum_recv.at[4 + which],
                device_id=peer,
                device_id_type=MESH,
            ).start()

    def sum_end(which):
        whole_wait(got_b.at[which, pl.ds(0, n_b - 1)], sum_recv.at[4 + which])
        total = got_b[which, 0]
        for slot in range(1, n_b):
            total = total + got_b[which, slot]
        sums = jnp.sum(total, axis=1, keepdims=True)
        return [sums[row : row + 1, :] for row in range(8)]

    def block_pass(blocks, vectors, emit):
        def body(group, _):
            sums = [None] * 8
            for block, vector in zip(blocks, vectors):
                values = vector[...]
                for row in range(8):
                    got = fold(block(group * 8 + row).astype(F32) * values)
                    sums[row] = got if sums[row] is None else sums[row] + got
            emit(pl.ds(pl.multiple_of(group * 8, 8), 8), merge_rows(sums))
            return 0

        lax.fori_loop(0, B // 8, body, 0, unroll=len(blocks) == 1)

    def spread(array, at):
        array = jnp.where(position == at, array, 0.0)
        for step in (LINES, 2 * LINES, 4 * LINES):
            array = array + pltpu.roll(array, step, 1)
        return array

    line_mask = [jnp.where(lane % LINES == m, 1.0, 0.0).astype(BF16) for m in range(LINES)]

    def stacked(vector):
        upper_half = vector.astype(BF16)
        lower_half = (vector - upper_half.astype(F32)).astype(BF16)
        halves = [jnp.concatenate([half * mask for mask in line_mask], axis=0) for half in (upper_half, lower_half)]
        return jnp.concatenate(halves, axis=1)

    def apply_maps(maps, vectors):
        right = jnp.concatenate([stacked(vector) for vector in vectors], axis=0)
        both = jnp.dot(maps, right, preferred_element_type=F32)
        return both[:, :E] + both[:, E:]

    def place(base, rows, steps, way):
        total = jnp.zeros((B, E), F32)
        for index, step in enumerate(steps):
            at = step if way == 0 else Q - 1 - step
            total = jnp.where(position == at, rows[index * B : index * B + B], total)
        return base + total

    def pack(array):
        total = array[0:8]
        for row in range(1, 8):
            total = jnp.where(lane8 // LINES == row, array[8 * row : 8 * row + 8], total)
        return total

    row_group = iota((B, E), 0) // 8

    def unpack(array):
        array = jnp.where(position == row_group, jnp.concatenate([array] * 8, axis=0), 0.0)
        for step in (LINES, 2 * LINES, 4 * LINES):
            array = array + pltpu.roll(array, step, 1)
        return array

    row32 = iota((32, E), 0)
    lane32 = iota((32, E), 1)
    selector = jnp.where(lane32 // 4 == row32, 1.0, 0.0).astype(BF16)
    quarter = [jnp.where(lane % 4 == m, 1.0, 0.0).astype(BF16) for m in range(4)]
    column_part = iota((B, 256), 1) // B
    column_mask = [jnp.where(column_part == m, 1.0, 0.0).astype(BF16) for m in range(4)]

    def turn(blocks):
        def body(i, _):
            rows = blocks[i]
            stack = jnp.concatenate([rows * quarter[m] for m in range(4)], axis=0)
            got = lax.dot_general(selector, stack, (((1,), (1,)), ((), ())), preferred_element_type=F32)
            turned[0, pl.ds(i, 32, stride=B), :] = got[:, :E]
            turned[1, pl.ds(i, 32, stride=B), :] = got[:, E:]
            return 0

        lax.fori_loop(0, B, body, 0, unroll=16)

    def matrix(way, step, group):
        at = step if way == 0 else Q - 1 - step
        rows = pl.ds((at * 4 + group) * B, B)
        return jnp.concatenate([turned[0, rows, :], turned[1, rows, :]], axis=1)

    def diagonal(array):
        return jnp.concatenate([array * column_mask[m] for m in range(4)], axis=0)

    def columns(group):
        return pl.ds(group * 256, 256)

    def build(way):
        for group in range(4):
            first = [None] * HALF
            second = [None] * HALF
            for step in range(HALF):
                for store, at in ((first, step), (second, HALF + step)):
                    mine = matrix(way, at, group)
                    if step == 0:
                        store[step] = (-mine).astype(BF16)
                    else:
                        store[step] = -jnp.dot(
                            mine.astype(BF16), diagonal(store[step - 1]), preferred_element_type=F32
                        )
                        store[step] = store[step].astype(BF16)
            for step in range(HALF):
                prefix_map[way, step * B : step * B + B, columns(group)] = first[step]
                chunk_map[way, step * B : step * B + B, columns(group)] = second[step]
            later = jnp.dot(chunk_map[way, :, columns(group)], diagonal(first[-1]), preferred_element_type=F32)
            prefix_map[way, HALF * B :, columns(group)] = later.astype(BF16)

    def build_both():
        for group in range(4):
            last = prefix_map[0, (Q - 1) * B :, columns(group)]
            both_map[(Q - 1) * B :, columns(group)] = last
            for at in reversed(range(Q - 1)):
                got = jnp.dot(
                    matrix(1, Q - 1 - at, group).astype(BF16), diagonal(last), preferred_element_type=F32
                )
                last = (prefix_map[0, at * B : at * B + B, columns(group)].astype(F32) - got).astype(BF16)
                both_map[at * B : at * B + B, columns(group)] = last

    def sweep(blocks, way):
        starts = position % HALF == (0 if way == 0 else HALF - 1)
        shift = LINES if way == 0 else E - LINES
        base = source[...]
        now = base
        for _ in range(HALF - 1):
            vecs[0] = jnp.where(starts, 0.0, pltpu.roll(now, shift, 1))

            def emit(rows, got):
                state[rows, :] = source[rows, :] - got

            block_pass([lambda i: blocks[i]], [vecs.at[0]], emit)
            now = state[...]
        last = HALF - 1 if way == 0 else HALF
        inflow = spread(now, last)
        end_rows = apply_maps(chunk_map[way, (HALF - 1) * B :, :], [inflow])
        end = spread(now, Q - 1 if way == 0 else 0) + end_rows

        def finish():
            rows = apply_maps(chunk_map[way, : (HALF - 1) * B, :], [inflow])
            whole = place(now, rows, range(HALF, Q - 1), way)
            return place(whole, end_rows, [Q - 1], way)

        return end, finish

    def exchange_start(index, way, end):
        ends[index] = pack(end)
        copies = {}
        for away in sorted(range(1, n_line), key=lambda n: -around(n_line, n)):
            copy = pltpu.make_async_remote_copy(
                src_ref=ends.at[index],
                dst_ref=got_ends.at[index, away - 1],
                send_sem=end_send.at[index, away - 1],
                recv_sem=end_recv.at[index, away - 1],
                device_id=peer_line(away if way == 0 else -away),
                device_id_type=MESH,
            )
            copy.start()
            copies[away] = copy
        return copies

    def entering(index, way, copies):
        room = line if way == 0 else n_line - 1 - line
        got = []
        for away in range(1, n_line):
            copies[away].wait_recv()
            got.append(unpack(jnp.where(room >= away, got_ends[index, away - 1], 0.0)))
        return got[0] + apply_maps(inflow_map[way], got[1:3])

    sent = []

    def precondition(iteration, after_send, after_solve):
        def emit(rows, got):
            source[rows, :] = got

        block_pass([lambda i: inv[i]], [vecs.at[0]], emit)
        end, finish = sweep(fwd, 0)
        copies = exchange_start(2 * iteration, 0, end)
        sent.extend(copies.values())
        values = finish()
        if iteration == 0:
            after_send()
            inflow = entering(0, 0, copies)
            source[...] = place(values, apply_maps(prefix_map[0], [inflow]), range(Q), 0)
            end, finish = sweep(bwd, 1)
            copies = exchange_start(1, 1, end)
            sent.extend(copies.values())
            values = finish()
            after_solve()
        else:
            source[...] = values
            end, finish = sweep(bwd, 1)
            values = finish()
            after_send()
            inflow = entering(2 * iteration, 0, copies)
            end = end + apply_maps(both_map[:B, :], [inflow])
            copies = exchange_start(2 * iteration + 1, 1, end)
            sent.extend(copies.values())
            values = place(values, apply_maps(both_map[...], [inflow]), range(Q), 0)
            after_solve()
        inflow = entering(2 * iteration + 1, 1, copies)
        return place(values, apply_maps(prefix_map[1], [inflow]), range(Q), 1), inflow

    def operate(iteration, values, inflow):
        rounded = values.astype(BF16)
        halo_out[iteration] = jnp.dot(rounded, send_pick[...], preferred_element_type=F32).astype(BF16)
        copies = []
        for slot, peer in enumerate((peer_dom(1), peer_dom(-1), peer_line(1))):
            copy = pltpu.make_async_remote_copy(
                src_ref=halo_out.at[iteration],
                dst_ref=got_halo.at[iteration, slot],
                send_sem=halo_send.at[iteration, slot],
                recv_sem=halo_recv.at[iteration, slot],
                device_id=peer,
                device_id_type=MESH,
            )
            copy.start()
            copies.append(copy)
        sent.extend(copies)
        vecs[0] = values
        vecs[1] = pltpu.roll(jnp.where(position == 0, inflow, values), E - LINES, 1)

        def emit_first(rows, got):
            state[rows, :] = got

        block_pass([lambda i: diag[i], lambda i: upper[i]], [vecs.at[0], vecs.at[1]], emit_first)
        rest = (values - rounded.astype(F32)).astype(BF16)
        here = jnp.dot(jnp.concatenate([rounded, rest], axis=0), pick[:E, :], preferred_element_type=F32)
        copies[2].wait_recv()
        behind = jnp.where(line > 0, got_halo[iteration, 2].astype(F32), 0.0)
        vecs[2] = pltpu.roll(jnp.where(position == Q - 1, behind, values), LINES, 1)

        def emit_more(rows, got):
            state[rows, :] = state[rows, :] + got

        block_pass([lambda i: lower[i]], [vecs.at[2]], emit_more)
        copies[0].wait_recv()
        copies[1].wait_recv()
        left = jnp.where(dom > 0, got_halo[iteration, 0].astype(F32), 0.0)
        right = jnp.where(dom < n_dom - 1, got_halo[iteration, 1].astype(F32), 0.0)
        received = jnp.where(lane < HALO, left, jnp.where(lane < 2 * HALO, right, 0.0)).astype(BF16)
        picked = here[:B] + here[B:] + jnp.dot(received, pick[E:, :], preferred_element_type=F32)
        for side in range(FACES):
            vecs[3 + side] = picked[:, side * E : side * E + E]

        def emit_second(rows, got):
            keep[6, rows, :] = state[rows, :] + got

        block_pass(
            [lambda i, side=side: face[side, i] for side in range(FACES)],
            [vecs.at[3 + side] for side in range(FACES)],
            emit_second,
        )

    loads[0].wait()
    turn(fwd)
    build(0)

    pl.semaphore_wait(barrier, len(partners))
    def rooms(way):
        return line if way == 0 else n_line - 1 - line

    def map_copy(way, away):
        return pltpu.make_async_remote_copy(
            src_ref=prefix_map.at[way, pl.ds((Q - 1) * B, B), :],
            dst_ref=got_map.at[way] if away == 2 else inflow_map.at[way, :, pl.ds(0, LINES * B)],
            send_sem=map_send.at[way, away - 1],
            recv_sem=map_recv.at[way, away - 1],
            device_id=peer_line(away if way == 0 else -away),
            device_id_type=MESH,
        )

    def sends_map(way, away):
        return (rooms(way) >= 1) & (rooms(way) + away < n_line)

    def send_maps(way):
        for away in (1, 2):

            @pl.when(sends_map(way, away))
            def _():
                map_copy(way, away).start()

    send_maps(0)
    loads[2].wait()
    vector = right_ref[...] * START_SCALE
    keep[3] = vector
    sum_start(0, [fold(vector * vector)])

    loads[3].wait()
    loads[4].wait()
    for side in range(FACES):
        hit = iota((256, E), 0) == nbr_ref[side : side + 1, :]
        pick[:, side * E : side * E + E] = jnp.where(hit, 1.0, 0.0).astype(BF16)
    lists[...] = jnp.zeros((8, E), jnp.int32)
    lists[0:1, 0:HALO] = send_ref[0:1, :]
    lists[1:2, 0:HALO] = send_ref[1:2, :]
    now = lists[...]
    moved = pltpu.roll(now, HALO, 1)
    lane_row = lane8[0:1]
    wanted = jnp.where(
        lane_row < HALO,
        now[0:1],
        jnp.where(lane_row < 2 * HALO, moved[1:2], jnp.where(lane_row >= (Q - 1) * LINES, lane_row, -1)),
    )
    send_pick[...] = jnp.where(iota((E, E), 0) == wanted, 1.0, 0.0).astype(BF16)

    loads[5].wait()

    def first_after_send():
        loads[1].wait()
        turn(bwd)
        build(1)
        send_maps(1)
        join_maps(0)
        sum_middle(0)

    def first_after_solve():
        build_both()
        join_maps(1)

    def join_maps(way):
        @pl.when(rooms(way) >= 2)
        def _():
            map_copy(way, 1).wait_recv()

        @pl.when(rooms(way) >= 3)
        def _():
            map_copy(way, 2).wait_recv()
            for group in range(4):
                near = inflow_map[way, :, columns(group)]
                both = jnp.dot(near, diagonal(got_map[way, :, columns(group)]), preferred_element_type=F32)
                inflow_map[way, :, columns(4 + group)] = both.astype(BF16)

    vecs[0] = vector
    values, inflow = precondition(0, first_after_send, first_after_solve)
    norm = jnp.sqrt(sum_end(0)[0])
    start_norm = norm * (1.0 / START_SCALE)
    search = values / norm
    keep[0] = search
    keep[3] = keep[3] / norm
    keep[7] = inflow / norm
    for slot in range(6, 10):
        loads[slot].wait()
    operate(0, search, keep[7])
    w = keep[6]
    first = keep[3]
    sum_start(1, [fold(w * first), fold(w * w)])

    vecs[0] = w * W_SCALE
    values, inflow = precondition(1, lambda: sum_middle(1), lambda: None)
    s = sum_end(1)
    tiny = 1e-14
    h11 = s[0]
    g1 = jnp.sqrt(jnp.maximum(s[1] - h11 * h11, tiny * s[1]))
    turn_back = 1.0 / W_SCALE
    first = keep[3]
    second = (keep[6] - h11 * first) / g1
    keep[4] = second
    search = (values / g1) * turn_back - (h11 / g1) * keep[0]
    entry = (inflow / g1) * turn_back - (h11 / g1) * keep[7]
    keep[1] = search
    keep[8] = entry
    operate(1, search, entry)
    w = keep[6]
    first = keep[3]
    second = keep[4]
    sum_start(2, [fold(w * first), fold(w * second), fold(w * w), fold(first * second), fold(second * second)])

    vecs[0] = w * W_SCALE
    values, inflow = precondition(2, lambda: sum_middle(2), lambda: None)
    s = sum_end(2)
    size2 = jnp.sqrt(s[4])
    h21 = g1 * size2
    h12 = s[0] / size2
    cross12 = s[3] / size2
    along2 = s[1] / (size2 * size2)
    h22 = along2 - h12 * cross12
    all2 = s[2] / (size2 * size2)
    rest2 = all2 + h12 * h12 + h22 * h22 - 2.0 * h12 * h12 - 2.0 * h22 * along2 + 2.0 * h12 * h22 * cross12
    g2 = jnp.sqrt(jnp.maximum(rest2, tiny * all2))
    from_w = 1.0 / (size2 * g2)
    from_1 = h12 / g2
    from_2 = h22 / (size2 * g2)
    third = from_w * keep[6] - from_1 * keep[3] - from_2 * keep[4]
    keep[5] = third
    search = (from_w * values) * turn_back - from_1 * keep[0] - from_2 * keep[1]
    entry = (from_w * inflow) * turn_back - from_1 * keep[7] - from_2 * keep[8]
    keep[2] = search
    operate(2, search, entry)
    w = keep[6]
    first = keep[3]
    second = keep[4]
    third = keep[5]
    sum_start(
        3,
        [
            fold(w * first),
            fold(w * second),
            fold(w * third),
            fold(w * w),
            fold(first * third),
            fold(second * third),
            fold(third * third),
        ],
    )
    sum_middle(3)
    s = sum_end(3)
    size3 = jnp.sqrt(s[6])
    h32 = g2 * size3
    h13 = s[0] / size3
    along2 = s[1] / (size3 * size2)
    along3 = s[2] / (size3 * size3)
    all3 = s[3] / (size3 * size3)
    cross13 = s[4] / size3
    cross23 = s[5] / (size3 * size2)
    h23 = along2 - h13 * cross12
    h33 = along3 - h13 * cross13 - h23 * cross23
    rest3 = (
        all3
        + h13 * h13
        + h23 * h23
        + h33 * h33
        - 2.0 * (h13 * h13 + h23 * along2 + h33 * along3)
        + 2.0 * (h13 * h23 * cross12 + h13 * h33 * cross13 + h23 * h33 * cross23)
    )
    h43 = jnp.sqrt(jnp.maximum(rest3, 0.0))

    n11 = h11 * h11 + h21 * h21
    n21 = h11 * h12 + h21 * h22
    n31 = h11 * h13 + h21 * h23
    n22 = h12 * h12 + h22 * h22 + h32 * h32
    n32 = h12 * h13 + h22 * h23 + h32 * h33
    n33 = h13 * h13 + h23 * h23 + h33 * h33 + h43 * h43
    l11 = jnp.sqrt(n11)
    l21 = n21 / l11
    l31 = n31 / l11
    l22 = jnp.sqrt(n22 - l21 * l21)
    l32 = (n32 - l31 * l21) / l22
    l33 = jnp.sqrt(n33 - l31 * l31 - l32 * l32)
    f1 = start_norm * h11 / l11
    f2 = (start_norm * h12 - l21 * f1) / l22
    f3 = (start_norm * h13 - l31 * f1 - l32 * f2) / l33
    c3 = f3 / l33
    c2 = (f2 - l32 * c3) / l22
    c1 = (f1 - l21 * c2 - l31 * c3) / l11
    update_ref[...] = c1 * keep[0] + (c2 / size2) * keep[1] + (c3 / size3) * keep[2]
    entries = {
        (0, 0): h11,
        (1, 0): h21,
        (0, 1): h12,
        (1, 1): h22,
        (2, 1): h32,
        (0, 2): h13,
        (1, 2): h23,
        (2, 2): h33,
        (3, 2): h43,
    }
    table = jnp.zeros((8, E), F32)
    sub8 = iota((8, E), 0)
    for (row, column), value in entries.items():
        table = jnp.where((sub8 == row) & (lane8 == column), value, table)
    hess_ref[...] = table[0 : ITERS + 1, 0:ITERS]

    for copy in sent:
        copy.wait_send()
    for way in range(2):
        for away in (1, 2):

            @pl.when(sends_map(way, away))
            def _():
                map_copy(way, away).wait_send()

    for which in range(4):
        whole_wait(got_a.at[which, pl.ds(0, n_a - 1)], sum_send.at[which])
        whole_wait(got_b.at[which, pl.ds(0, n_b - 1)], sum_send.at[4 + which])


def shards(sizes, right_side, diag, lower, upper, face, nbr, send, inv, fwd, bwd):
    n_dom, n_line, high, low = sizes
    n_a, n_b = n_line * high, low
    vmem = pl.BlockSpec(memory_space=pltpu.VMEM)
    hbm = pl.BlockSpec(memory_space=pltpu.HBM)
    block = pltpu.VMEM((B, B, E), BF16)
    dma = pltpu.SemaphoreType.DMA
    update, hess = pl.pallas_call(
        functools.partial(kernel, sizes),
        out_shape=(jax.ShapeDtypeStruct((B, E), F32), jax.ShapeDtypeStruct((ITERS + 1, ITERS), F32)),
        in_specs=[hbm] * 10,
        out_specs=(vmem, vmem),
        scratch_shapes=[
            pltpu.VMEM((B, E), F32),
            pltpu.VMEM((FACES, E), jnp.int32),
            pltpu.VMEM((2, HALO), jnp.int32),
            block,
            block,
            block,
            pltpu.VMEM((FACES, B, B, E), BF16),
            block,
            block,
            block,
            pltpu.VMEM((2, 32 * B, E), F32),
            pltpu.VMEM((2, Q * B, LINES * B), BF16),
            pltpu.VMEM((2, HALF * B, LINES * B), BF16),
            pltpu.VMEM((Q * B, LINES * B), BF16),
            pltpu.VMEM((2, B, LINES * B), BF16),
            pltpu.VMEM((2, B, 2 * LINES * B), BF16),
            pltpu.VMEM((256, FACES * E), BF16),
            pltpu.VMEM((E, E), BF16),
            pltpu.VMEM((8, E), jnp.int32),
            pltpu.VMEM((3 + FACES, B, E), F32),
            pltpu.VMEM((B, E), F32),
            pltpu.VMEM((B, E), F32),
            pltpu.VMEM((9, B, E), F32),
            pltpu.VMEM((6, 8, E), F32),
            pltpu.VMEM((6, 3, 8, E), F32),
            pltpu.VMEM((3, B, E), BF16),
            pltpu.VMEM((3, 3, B, E), BF16),
            pltpu.VMEM((8, 8, E), F32),
            pltpu.VMEM((4, n_a, 8, E), F32),
            pltpu.VMEM((4, n_b, 8, E), F32),
            dma((10,)),
            dma((2, 2)),
            dma((2, 2)),
            dma((6, 3)),
            dma((6, 3)),
            dma((3, 3)),
            dma((3, 3)),
            dma((8,)),
            dma((8,)),
        ],
        compiler_params=pltpu.CompilerParams(
            collective_id=0, has_side_effects=True, vmem_limit_bytes=64 * 1024 * 1024
        ),
    )(right_side, nbr, send, diag, lower, upper, face, inv, fwd, bwd)
    return update, hess


def solution(mesh):
    n_dom, n_line = mesh.shape["dom"], mesh.shape["line"]
    low = 16 if n_dom >= 32 else 2
    sizes = (n_dom, n_line, n_dom // low, low)
    both = ("dom", "line")
    in_specs = (
        P(None, both),
        P(None, None, both),
        P(None, None, both),
        P(None, None, both),
        P(None, None, None, both),
        P(None, both),
        P(None, both),
        P(None, None, both),
        P(None, None, both),
        P(None, None, both),
    )
    return jax.shard_map(
        functools.partial(shards, sizes),
        mesh=mesh,
        in_specs=in_specs,
        out_specs=(P(None, both), P()),
        check_vma=False,
    )
```

time: 1150 us -> 78 us (0.07); the launches traced: 1130 us -> 77.8 us
  blocking collectives: 825 us -> 0 us
  matrix products: 138 us -> 0 us
  other arithmetic: 77.9 us -> 0 us
  Pallas kernels: 0 us -> 74.5 us
  starting transfers between devices: 49.9 us -> 0 us
  local copies, waits for them, and re-layouts: 36.1 us -> 2.62 us
    psum x10 -> x0, blocking collectives: 747 us -> none  [the longest x6 445 us: shards(): weight_ij = lax.psum(jnp.sum(product_vec * krylov[column]), ('dom', 'line'))]
    dot_general x130 -> x0, matrix products: 138 us -> none  [the longest x113 125 us: couple(): jnp.einsum('ijl,jl->il', blocks.astype(jnp.float32), carried, precision=H...]
    all_gather x8 -> x0, blocking collectives: 78 us -> none  [the longest x4 39.9 us: prefix(): lax.all_gather(part.astype(kind), axis)]
    pallas_call x0 -> x1, Pallas kernels: none -> 74.5 us  [shards(): pl.pallas_call(functools.partial(kernel, sizes), out_shape=(jax.ShapeDtyp...]
    ppermute x12 -> x0, starting transfers between devices: 49.9 us -> none  [the longest x6 40 us: from_behind(): return lax.ppermute(block, axis, route)]
    sub x84 -> x0, other arithmetic: 32.7 us -> none  [the longest x42 28.2 us: sweep_down(): carried = source[:, position] - couple(blocks[:, :, position], carried)]
    dot_general x12 -> x0, other arithmetic: 22.2 us -> none  [the longest x9 12.3 us: apply_blocks(): jnp.einsum('ije,je->ie', blocks, rounded, preferred_element_type=jnp.floa...]
    unnamed x95 -> x2, local copies, waits for them, and re-layouts: 14.2 us -> 2.62 us
  transfers between devices with their start and end apart: 12 -> 0, of which waited for: 0 -> 0; matrix products, arithmetic and copies ran while one was open for 2% -> 0% of each run, Pallas kernels for 0% -> 0%
where the time goes in v1:
time: 78 us; the launch traced here: 77.8 us
  Pallas kernels  74.5 us (96%)
  local copies, waits for them, and re-layouts  2.62 us (3%)
    pallas_call x1, Pallas kernels, shards(): pl.pallas_call(functools.partial(kernel, sizes), out_shape=(jax.ShapeDtyp...  74.5 us
    unnamed x2, local copies, waits for them, and re-layouts  2.62 us

profile of v1, /device:TPU:1, one launch (start us, length us, event | category | flops | bytes accessed | tf_op | source)
XLA Modules:
  0.0 77.8 jit_solution(12156044229817859970)
XLA Ops:
  0.6 74.5 %shard_map.113 = (f32[64,128]{1,0:T(8,128)}, f32[4,3]{1,0:T(4,128)}) custom-call(f32[64,128]{1,0:T(8,128)} %right_hbm.1, s32[4,128]{1,0:T(4,128)} %nbr_hbm.1, s32[2,16]{1,0:T(2,128)} %send_hbm.1, bf16[64,64,128]{2,1,0:T(8,128)(2,1)} %diag_hbm.1, bf16[64,64,128]{2,1,0:T(8,128)(2,1)} %lower_hbm.1, bf16[64,64,128]{2,1,0:T(8,128)(2,1)} %upper_hbm.1, ...), custom_call_target="tpu_custom_call" | custom-call | tf_op jit(solution)/shard_map/pallas_call | solution.py:709
  75.2 1.4 %copy.14 = f32[64,128]{1,0:T(8,128)} copy(f32[64,128]{1,0:T(8,128)} %get-tuple-element.4) | data formatting | bytes 65536
  76.5 1.2 %copy.15 = f32[4,3]{1,0:T(4,128)} copy(f32[4,3]{1,0:T(4,128)} %get-tuple-element.5) | data formatting | bytes 96
